TPU v7x, 32 devices: a whole 2x2x4 slice. The times are simulated.
32 devices in a mesh: parts: 2 (over y), ckpt: 4 (over x, core), dp: 4 (over z).
Axes of the slice: x: 2, y: 2, z: 4, core: 2. Of those that a mesh axis runs over, the one named last changes fastest.
Arguments:
- train_grads: bfloat16 [4, 8192, 4096], P('ckpt', ('parts', 'dp')), parts along dimension 1, may hold values from -6 to 6
- query_slots: bfloat16 [4, 4, 256, 4096], P('ckpt', 'dp'), may hold values from -0.09375 to 0.09375
- owners: int32 [4], replicated, may hold values from 0 to 3, as said below
- lr_weights: float32 [4], P('ckpt'), may hold values from 0.3 to 3
Outputs:
- scores: float32 [1024, 8192], P('ckpt', ('parts', 'dp')), parts along dimension 1
There are 2 independent parts, one for each index of `parts`. A program takes and returns all parts, laid end to end along the dimension named above; an argument that names none is the same for every part. Nothing has to cross between parts.
Inputs may be any that keep to these rules, and one draw needn't show every extreme that they name: The 4 owners are distinct.
All inputs are finite; a program needn't handle non-finite values.
Results may differ from a plain program's by a relative error of at most 0.0003.
Values may be sent and summed in bfloat16 or wider, within the bound.
A program may use at most 128 MiB of HBM per device.

v0:
```python
import jax
import jax.numpy as jnp
from jax import lax
from jax.sharding import PartitionSpec as P

GROUPS = 4


def from_root(block, axis, holder):
    block = jnp.where(lax.axis_index(axis) == holder, block, jnp.zeros_like(block))
    return lax.psum(block, axis)


def weighted_scores(block, grads, weight):
    product = lax.dot_general(
        block, grads, (((1,), (1,)), ((), ())), preferred_element_type=jnp.float32
    )
    return weight * product


def per_device(train_grads, query_slots, owners, lr_weights):
    grads = train_grads[0]
    slot = query_slots[0, 0]
    weight = lr_weights[0]
    blocks = []
    for step in range(GROUPS):
        blocks.append(from_root(slot, "dp", owners[step]))
    queries = jnp.concatenate(blocks, axis=0)
    term = weighted_scores(queries, grads, weight)
    return lax.psum_scatter(term, "ckpt", scatter_dimension=0, tiled=True)


def solution(mesh):
    placed = (P("ckpt", ("parts", "dp"), None), P("ckpt", "dp", None, None), P(), P("ckpt"))
    return jax.shard_map(
        per_device,
        mesh=mesh,
        in_specs=placed,
        out_specs=P("ckpt", ("parts", "dp")),
        check_vma=False,
    )
```

profile of v0, /device:TPU:17, one launch (start us, length us, event | category | flops | bytes accessed | tf_op | source)
XLA Modules:
  0.0 377.1 jit_solution(14603431332218989874)
XLA Ops:
  6.5 0.0 all-reduce.3.cloned.1.call-start
  6.5 1.5 fusion.15
  10.5 5.0 %select_bitcast_fusion.3 = (bf16[256,4096]{1,0:T(8,128)(2,1)}, bf16[256,4096]{1,0:T(8,128)(2,1)}, bf16[256,4096]{1,0:T(8,128)(2,1)}, bf16[256,4096]{1,0:T(8,128)(2,1)}) fusion(bf16[1,1,256,4096]{3,2,1,0:T(8,128)(2,1)} %param.5, pred[]{:T(512)S(6)} %eq.12, pred[]{:T(512)S(6)} %eq.13, pred[]{:T(512)S(6)} %eq.15, pred[]{:T(512)S(6)} %eq.14), kind=kLoop, calls=%fused_computation.13 | loop fusion | flops 4194304 | bytes 10485764 | tf_op jit(solution)/shard_map/jit(_where)/select_n | solution.py:10
  15.5 0.0 all-reduce.3.cloned.1.call-update
  15.5 0.0 reduce-scatter.2.cloned.1.call-start
  16.2 292.3 %all-reduce.3.cloned.1.call-done = (bf16[256,4096]{1,0:T(8,128)(2,1)}, bf16[256,4096]{1,0:T(8,128)(2,1)}, bf16[256,4096]{1,0:T(8,128)(2,1)}, bf16[256,4096]{1,0:T(8,128)(2,1)}) async-done(((bf16[256,4096]{1,0:T(8,128)(2,1)}, bf16[256,4096]{1,0:T(8,128)(2,1)}, bf16[256,4096]{1,0:T(8,128)(2,1)}, bf16[256,4096]{1,0:T(8,128)(2,1)}), (bf16[256,4096]{1,0:T(8,128)(2,1)}, bf16[256,4096]{1,0:T(8,128)(2,1)}, ...) | async-done | bytes 8388624 | tf_op jit(solution)/shard_map/psum | solution.py:11
  308.5 17.0 %fusion.9 = f32[1024,1024]{1,0:T(8,128)} fusion(bf16[1,1024,4096]{2,1,0:T(8,128)(2,1)} %param.4, bf16[256,4096]{1,0:T(8,128)(2,1)} %get-tuple-element.5, bf16[256,4096]{1,0:T(8,128)(2,1)} %get-tuple-element.6, bf16[256,4096]{1,0:T(8,128)(2,1)} %get-tuple-element.7, bf16[256,4096]{1,0:T(8,128)(2,1)} %get-tuple-element.8, f32[]{:T(128)} %bitcast.18), kind=kOutput, calls=%fused_computation.9 | convolution fusion | flops 8624537600 | bytes 20971524 | tf_op jit(solution)/shard_map/dot_general | solution.py:15
  325.6 0.0 reduce-scatter.2.cloned.1.call-update
  325.6 44.7 %reduce-scatter.2.cloned.1.call-done = f32[256,1024]{1,0:T(8,128)} async-done(((f32[1024,1024]{1,0:T(8,128)}), f32[256,1024]{1,0:T(8,128)}) %reduce-scatter.2.cloned.1.call-update) | async-done | bytes 1048592 | tf_op jit(solution)/shard_map/reduce_scatter | solution.py:30
Async XLA Ops:
  6.5 302.0 %all-reduce.3.cloned.1.call-start = ((), (), s32[]{:S(2)}) async-start(), calls=%async_computation.2 | async-start | bytes 16777216 | tf_op jit(solution)/shard_map/psum | solution.py:11
  15.5 354.7 %reduce-scatter.2.cloned.1.call-start = ((), (), s32[]{:S(2)}) async-start(), calls=%async_computation.1 | async-start | bytes 5242880 | tf_op jit(solution)/shard_map/reduce_scatter | solution.py:30
Sparse Core Ops, SparseCore 0:
  15.6 292.8 all-reduce.2
  325.7 44.4 reduce-scatter.1
where the time goes:
time: 379 us; the launch traced here: 377 us
  waiting for transfers between devices  337 us (89%)
  matrix products  17 us (4%)
  between operations  16.6 us (4%)
  other arithmetic  4.96 us (1%)
    psum x1, waiting for transfers between devices, from_root(): return lax.psum(block, axis)  292 us
    reduce_scatter x1, waiting for transfers between devices, per_device(): return lax.psum_scatter(term, 'ckpt', scatter_dimension=0, tiled=True)  44.7 us
    dot_general x1, matrix products, weighted_scores(): lax.dot_general(block, grads, (((1,), (1,)), ((), ())), preferred_element...  17 us
  transfers between devices with their start and end apart: 2, of which 2 were waited for; matrix products, arithmetic and copies ran while one was open for 0% of the time, Pallas kernels for 0%

commit v1 on v0

--- a/solution.py
+++ b/solution.py
@@ -1,9 +1,15 @@
+import functools
+
 import jax
 import jax.numpy as jnp
 from jax import lax
+from jax.experimental import pallas as pl
+from jax.experimental.pallas import tpu as pltpu
 from jax.sharding import PartitionSpec as P
 
 GROUPS = 4
+CHUNK = 32
+MESH = pl.DeviceIdType.MESH
 
 
 def from_root(block, axis, holder):
@@ -30,10 +36,285 @@
     return lax.psum_scatter(term, "ckpt", scatter_dimension=0, tiled=True)
 
 
+def slot_kernel(
+    grads_hbm, slot_hbm, weight_ref, out_ref,
+    q, g, term, core_in, pair, x_in, final,
+    load_sem, right_sem, left_sem, z_sem, y_send, y_sem,
+    a_send, a_recv, b_send, b_recv, c_send, c_recv, store_sem,
+):
+    slots, rows, _ = q.shape
+    half = term.shape[-1]
+    chunks = rows // (2 * CHUNK)
+    steps = (slots - 1) * chunks
+    y, j, z = lax.axis_index("parts"), lax.axis_index("ckpt"), lax.axis_index("dp")
+    x, c = lax.div(j, 2), lax.rem(j, 2)
+    other_y = {"parts": 1 - y}
+    other_core = {"ckpt": 2 * x + 1 - c}
+    other_x = {"ckpt": 2 * (1 - x) + c}
+    right, left = {"dp": z + 1}, {"dp": z - 1}
+    has_right, has_left = z < slots - 1, z > 0
+
+    def loads():
+        return (
+            pltpu.make_async_copy(slot_hbm, q.at[z], load_sem.at[0]),
+            pltpu.make_async_copy(grads_hbm, g, load_sem.at[1]),
+        )
+
+    def sent(i, of):
+        return pl.ds(pl.multiple_of(i * 2 * CHUNK + of * CHUNK, CHUNK), CHUNK)
+
+    def remote(src, dst, send, recv, device):
+        return pltpu.make_async_remote_copy(
+            src_ref=src, dst_ref=dst, send_sem=send, recv_sem=recv, device_id=device, device_id_type=MESH
+        )
+
+    def to_right(s, i, src=None):
+        block = q.at[s, sent(i, y)]
+        return remote(block if src is None else src, block, right_sem.at[s, i], z_sem.at[s, i], right)
+
+    def to_left(s, i, src=None):
+        block = q.at[s, sent(i, y)]
+        return remote(block if src is None else src, block, left_sem.at[s, i], z_sem.at[s, i], left)
+
+    def to_y(s, i):
+        block = q.at[s, sent(i, y)]
+        return remote(block, block, y_send.at[s, i], y_sem.at[s, i], other_y)
+
+    far = lax.div(z, 2)
+    near = z + far * (slots - 1 - 2 * z)
+
+    def slot_of(p):
+        k = lax.div(p, chunks) + 1
+        later = lax.div(k + 2, 4)
+        f = (1 - later) * (1 - near) + later * k
+        return f + far * (slots - 1 - 2 * f)
+
+    def place(p):
+        if isinstance(p, int):
+            return z, slice(None), 0
+        i = lax.rem(p, chunks)
+        return slot_of(p), pl.ds(pl.multiple_of(i * 2 * CHUNK, 2 * CHUNK), 2 * CHUNK), p + 1
+
+    def core_copy(p):
+        s, r, n = place(p)
+        return remote(term.at[s, 1 - c, r], core_in.at[s, r], a_send.at[n], a_recv.at[n], other_core)
+
+    def x_copy(p):
+        s, r, n = place(p)
+        return remote(pair.at[s, r], x_in.at[s, r], b_send.at[n], b_recv.at[n], other_x)
+
+    def final_copies(p):
+        s, r, n = place(p)
+        mine = pl.ds(pl.multiple_of(c * half, half), half)
+        dst = out_ref.at[s, r, mine]
+        return (
+            remote(final.at[s, r], dst, c_send.at[n], c_recv.at[n], other_core),
+            pltpu.make_async_copy(final.at[s, r], dst, store_sem.at[n]),
+        )
+
+    def arrived_final(p):
+        s, r, n = place(p)
+        theirs = pl.ds(pl.multiple_of((1 - c) * half, half), half)
+        return remote(final.at[s, r], out_ref.at[s, r, theirs], c_send.at[n], c_recv.at[n], other_core)
+
+    def multiply(p):
+        s, r, _ = place(p)
+        for step in range(2):
+            h = (1 - c) if step == 0 else c
+            columns = pl.ds(pl.multiple_of(h * half, half), half)
+            product = lax.dot_general(
+                q[s, r], g[columns], (((1,), (1,)), ((), ())), preferred_element_type=jnp.float32
+            )
+            term[s, h, r] = weight_ref[0] * product
+            if step == 0:
+                core_copy(p).start()
+
+    def add_core(p):
+        s, r, _ = place(p)
+        core_copy(p).wait_recv()
+        pair[s, r] = term[s, c, r] + core_in[s, r]
+        x_copy(p).start()
+
+    def add_x(p):
+        s, r, _ = place(p)
+        x_copy(p).wait_recv()
+        final[s, r] = pair[s, r] + x_in[s, r]
+        for copy in final_copies(p):
+            copy.start()
+
+    for load in loads():
+        load.start()
+
+    barrier = pltpu.get_barrier_semaphore()
+    for device in (other_y, other_core, other_x):
+        pl.semaphore_signal(barrier, inc=1, device_id=device, device_id_type=MESH)
+    for has, device in ((has_right, right), (has_left, left)):
+
+        @pl.when(has)
+        def _():
+            pl.semaphore_signal(barrier, inc=1, device_id=device, device_id_type=MESH)
+
+    pl.semaphore_wait(barrier, 3 + lax.div(z + slots - 1, slots) + 1 - lax.div(z + 1, slots))
+
+    for i in range(chunks):
+        src = slot_hbm.at[sent(i, y)]
+
+        @pl.when(has_right)
+        def _():
+            to_right(z, i, src).start()
+
+        @pl.when(has_left)
+        def _():
+            to_left(z, i, src).start()
+
+    def forward(n):
+        t, i = lax.div(n, chunks), lax.rem(n, chunks)
+
+        @pl.when(z - 1 - t >= 0)
+        def _():
+            s = z - 1 - t
+            to_right(s, i).wait_recv()
+            to_y(s, i).start()
+
+            @pl.when(has_right)
+            def _():
+                to_right(s, i).start()
+
+        @pl.when(z + 1 + t < slots)
+        def _():
+            s = z + 1 + t
+            to_left(s, i).wait_recv()
+            to_y(s, i).start()
+
+            @pl.when(has_left)
+            def _():
+                to_left(s, i).start()
+
+    forward(jnp.int32(0))
+    for load in loads():
+        load.wait()
+    multiply(-1)
+
+    def body(n, carry):
+        @pl.when(n < steps)
+        def _():
+            forward(n)
+
+        @pl.when(n == 1)
+        def _():
+            add_core(-1)
+
+        @pl.when(n == 2)
+        def _():
+            add_x(-1)
+
+        @pl.when(n <= steps)
+        def _():
+            p = n - 1
+            to_y(slot_of(p), lax.rem(p, chunks)).wait_recv()
+            multiply(p)
+
+        @pl.when(jnp.logical_and(n >= 2, n <= steps + 1))
+        def _():
+            add_core(n - 2)
+
+        @pl.when(n >= 3)
+        def _():
+            add_x(n - 3)
+
+        return carry
+
+    lax.fori_loop(1, steps + 3, body, 0)
+
+    def finish(p):
+        core_copy(p).wait_send()
+        x_copy(p).wait_send()
+        arrived_final(p).wait_recv()
+        sent_copy, stored = final_copies(p)
+        sent_copy.wait_send()
+        stored.wait()
+
+    finish(-1)
+
+    def finish_step(p, carry):
+        to_y(slot_of(p), lax.rem(p, chunks)).wait_send()
+        finish(p)
+        return carry
+
+    lax.fori_loop(0, steps, finish_step, 0)
+
+    def finish_sends(n, carry):
+        s, i = lax.div(n, chunks), lax.rem(n, chunks)
+
+        @pl.when(jnp.logical_and(has_right, s <= z))
+        def _():
+            to_right(s, i).wait_send()
+
+        @pl.when(jnp.logical_and(has_left, s >= z))
+        def _():
+            to_left(s, i).wait_send()
+
+        return carry
+
+    lax.fori_loop(0, slots * chunks, finish_sends, 0)
+
+
+def all_slots_owned(train_grads, query_slots, owners, lr_weights):
+    grads, slot = train_grads[0], query_slots[0, 0]
+    slots = GROUPS
+    rows, depth = slot.shape
+    columns = grads.shape[0]
+    chunks = rows // (2 * CHUNK)
+    items = (slots - 1) * chunks + 1
+    dma = pltpu.SemaphoreType.DMA
+    f32 = jnp.float32
+    scores = pl.pallas_call(
+        slot_kernel,
+        out_shape=jax.ShapeDtypeStruct((slots, rows, columns), f32),
+        in_specs=[
+            pl.BlockSpec(memory_space=pl.ANY),
+            pl.BlockSpec(memory_space=pl.ANY),
+            pl.BlockSpec(memory_space=pltpu.SMEM),
+        ],
+        out_specs=pl.BlockSpec(memory_space=pl.ANY),
+        scratch_shapes=[
+            pltpu.VMEM((slots, rows, depth), slot.dtype),
+            pltpu.VMEM((columns, depth), grads.dtype),
+            pltpu.VMEM((slots, 2, rows, columns // 2), f32),
+            pltpu.VMEM((slots, rows, columns // 2), f32),
+            pltpu.VMEM((slots, rows, columns // 2), f32),
+            pltpu.VMEM((slots, rows, columns // 2), f32),
+            pltpu.VMEM((slots, rows, columns // 2), f32),
+            dma((2,)),
+            dma((slots, chunks)),
+            dma((slots, chunks)),
+            dma((slots, chunks)),
+            dma((slots, chunks)),
+            dma((slots, chunks)),
+            dma((items,)),
+            dma((items,)),
+            dma((items,)),
+            dma((items,)),
+            dma((items,)),
+            dma((items,)),
+            dma((items,)),
+        ],
+        compiler_params=pltpu.CompilerParams(
+            collective_id=0, has_side_effects=True, vmem_limit_bytes=56 * 1024 * 1024
+        ),
+        cost_estimate=pl.CostEstimate(
+            flops=2 * slots * rows * columns * depth, bytes_accessed=16 << 20, transcendentals=0
+        ),
+    )(grads, slot, lr_weights)
+    return lax.dynamic_index_in_dim(scores, owners[lax.axis_index("ckpt")], 0, keepdims=False)
+
+
 def solution(mesh):
     placed = (P("ckpt", ("parts", "dp"), None), P("ckpt", "dp", None, None), P(), P("ckpt"))
+    sizes = dict(mesh.shape)
+    every = sizes["dp"] == GROUPS and sizes["ckpt"] == GROUPS and sizes["parts"] == 2
     return jax.shard_map(
-        per_device,
+        all_slots_owned if every else per_device,
         mesh=mesh,
         in_specs=placed,
         out_specs=P("ckpt", ("parts", "dp")),

time: 379 us -> 107 us (0.28)
  waiting for transfers between devices: 337 us -> 0 us
  Pallas kernels: 0 us -> 100 us
  matrix products: 17 us -> 0 us
  between operations: 16.6 us -> 2.6 us
  other arithmetic: 4.96 us -> 0 us
    psum x1 -> x0, waiting for transfers between devices: 292 us -> none  [from_root(): return lax.psum(block, axis)]
    pallas_call x0 -> x1, Pallas kernels: none -> 100 us  [all_slots_owned(): pl.pallas_call(slot_kernel, out_shape=jax.ShapeDtypeStruct((slots, rows,...]
    reduce_scatter x1 -> x0, waiting for transfers between devices: 44.7 us -> none  [per_device(): return lax.psum_scatter(term, 'ckpt', scatter_dimension=0, tiled=True)]
    dot_general x1 -> x0, matrix products: 17 us -> none  [weighted_scores(): lax.dot_general(block, grads, (((1,), (1,)), ((), ())), preferred_element...]
    select_n x1 -> x0, other arithmetic: 4.96 us -> none  [from_root(): jnp.where(lax.axis_index(axis) == holder, block, jnp.zeros_like(block))]
  transfers between devices with their start and end apart: 2 -> 0, of which waited for: 2 -> 0; matrix products, arithmetic and copies ran while one was open for 0% -> 0% of each run, Pallas kernels for 0% -> 0%
where the time goes in v1:
time: 107 us; the launch traced here: 106 us
  Pallas kernels  100 us (93%)
  local copies, waits for them, and re-layouts  3.55 us (3%)
  between operations  2.6 us (2%)
    pallas_call x1, Pallas kernels, all_slots_owned(): pl.pallas_call(slot_kernel, out_shape=jax.ShapeDtypeStruct((slots, rows,...  100 us
    squeeze x1, local copies, waits for them, and re-layouts, all_slots_owned(): lax.dynamic_index_in_dim(scores, owners[lax.axis_index('ckpt')], 0, keepd...  2.31 us

profile of v1, /device:TPU:17, one launch (start us, length us, event | category | flops | bytes accessed | tf_op | source)
XLA Modules:
  0.0 106.4 jit_solution(15083624570763286775)
XLA Ops:
  0.7 1.2 %dynamic_slice.7 = s32[1]{0:T(128)} dynamic-slice(s32[4]{0:T(128)} %param.6, s32[]{:T(128)S(6)} %select_n.7), dynamic_slice_sizes={1} | dynamic-slice | bytes 12 | tf_op jit(solution)/shard_map/dynamic_slice | solution.py:309
  3.8 100.2 %shard_map.46 = f32[4,256,1024]{2,1,0:T(8,128)} custom-call(bf16[1024,4096]{1,0:T(8,128)(2,1)} %bitcast.5, bf16[256,4096]{1,0:T(8,128)(2,1)} %bitcast.6, f32[1]{0:T(128)S(6)} %copy.5.weight_ref), custom_call_target="tpu_custom_call" | custom-call | flops 8589934592 | bytes 16777216 | tf_op jit(solution)/shard_map/pallas_call | solution.py:271
  104.0 2.3 %dynamic-slice_bitcast_fusion = f32[256,1024]{1,0:T(8,128)} fusion(f32[4,256,1024]{2,1,0:T(8,128)} %shard_map.46, s32[]{:T(128)S(6)} %select_n.8), kind=kLoop, calls=%fused_computation | loop fusion | bytes 2097156 | tf_op jit(solution)/shard_map/jit(dynamic_index_in_dim)/squeeze | solution.py:309

commit v2 on v1

--- a/solution.py
+++ b/solution.py
@@ -9,6 +9,10 @@
 
 GROUPS = 4
 CHUNK = 32
+TURN = 256
+LAG_Y = 2
+LAG_CORE = 2
+LAG_X = 2
 MESH = pl.DeviceIdType.MESH
 
 
@@ -38,7 +42,7 @@
 
 def slot_kernel(
     grads_hbm, slot_hbm, weight_ref, out_ref,
-    q, g, term, core_in, pair, x_in, final,
+    q, g, gt, term, core_in, pair, x_in, final,
     load_sem, right_sem, left_sem, z_sem, y_send, y_sem,
     a_send, a_recv, b_send, b_recv, c_send, c_recv, store_sem,
 ):
@@ -123,7 +127,7 @@
             h = (1 - c) if step == 0 else c
             columns = pl.ds(pl.multiple_of(h * half, half), half)
             product = lax.dot_general(
-                q[s, r], g[columns], (((1,), (1,)), ((), ())), preferred_element_type=jnp.float32
+                q[s, r], gt[:, columns], (((1,), (0,)), ((), ())), preferred_element_type=jnp.float32
             )
             term[s, h, r] = weight_ref[0] * product
             if step == 0:
@@ -193,6 +197,13 @@
     forward(jnp.int32(0))
     for load in loads():
         load.wait()
+
+    def turn(b, carry):
+        r = pl.ds(pl.multiple_of(b * TURN, TURN), TURN)
+        gt[:, r] = g[r].T
+        return carry
+
+    lax.fori_loop(0, g.shape[0] // TURN, turn, 0)
     multiply(-1)
 
     def body(n, carry):
@@ -200,31 +211,31 @@
         def _():
             forward(n)
 
-        @pl.when(n == 1)
+        @pl.when(n == 2)
         def _():
             add_core(-1)
 
-        @pl.when(n == 2)
+        @pl.when(n == 4)
         def _():
             add_x(-1)
 
-        @pl.when(n <= steps)
-        def _():
-            p = n - 1
+        @pl.when(jnp.logical_and(n >= LAG_Y, n < LAG_Y + steps))
+        def _():
+            p = n - LAG_Y
             to_y(slot_of(p), lax.rem(p, chunks)).wait_recv()
             multiply(p)
 
-        @pl.when(jnp.logical_and(n >= 2, n <= steps + 1))
-        def _():
-            add_core(n - 2)
-
-        @pl.when(n >= 3)
-        def _():
-            add_x(n - 3)
+        @pl.when(jnp.logical_and(n >= LAG_Y + LAG_CORE, n < LAG_Y + LAG_CORE + steps))
+        def _():
+            add_core(n - LAG_Y - LAG_CORE)
+
+        @pl.when(n >= LAG_Y + LAG_CORE + LAG_X)
+        def _():
+            add_x(n - LAG_Y - LAG_CORE - LAG_X)
 
         return carry
 
-    lax.fori_loop(1, steps + 3, body, 0)
+    lax.fori_loop(1, steps + LAG_Y + LAG_CORE + LAG_X, body, 0)
 
     def finish(p):
         core_copy(p).wait_send()
@@ -280,6 +291,7 @@
         scratch_shapes=[
             pltpu.VMEM((slots, rows, depth), slot.dtype),
             pltpu.VMEM((columns, depth), grads.dtype),
+            pltpu.VMEM((depth, columns), grads.dtype),
             pltpu.VMEM((slots, 2, rows, columns // 2), f32),
             pltpu.VMEM((slots, rows, columns // 2), f32),
             pltpu.VMEM((slots, rows, columns // 2), f32),

time: 107 us -> 99.9 us (0.934)
  Pallas kernels: 100 us -> 93.5 us
    pallas_call x1, Pallas kernels: 100 us -> 93.5 us  [all_slots_owned(): pl.pallas_call(slot_kernel, out_shape=jax.ShapeDtypeStruct((slots, rows,...]
where the time goes in v2:
time: 99.9 us; the launch traced here: 99.7 us
  Pallas kernels  93.5 us (94%)
  local copies, waits for them, and re-layouts  3.55 us (4%)
  between operations  2.6 us (3%)
    pallas_call x1, Pallas kernels, all_slots_owned(): pl.pallas_call(slot_kernel, out_shape=jax.ShapeDtypeStruct((slots, rows,...  93.5 us
    squeeze x1, local copies, waits for them, and re-layouts, all_slots_owned(): lax.dynamic_index_in_dim(scores, owners[lax.axis_index('ckpt')], 0, keepd...  2.31 us

profile of v2, /device:TPU:17, one launch (start us, length us, event | category | flops | bytes accessed | tf_op | source)
XLA Modules:
  0.0 99.7 jit_solution(1421705205240543916)
XLA Ops:
  0.7 1.2 %dynamic_slice.7 = s32[1]{0:T(128)} dynamic-slice(s32[4]{0:T(128)} %param.6, s32[]{:T(128)S(6)} %select_n.7), dynamic_slice_sizes={1} | dynamic-slice | bytes 12 | tf_op jit(solution)/shard_map/dynamic_slice | solution.py:321
  3.8 93.5 %shard_map.46 = f32[4,256,1024]{2,1,0:T(8,128)} custom-call(bf16[1024,4096]{1,0:T(8,128)(2,1)} %bitcast.5, bf16[256,4096]{1,0:T(8,128)(2,1)} %bitcast.6, f32[1]{0:T(128)S(6)} %copy.5.weight_ref), custom_call_target="tpu_custom_call" | custom-call | flops 8589934592 | bytes 16777216 | tf_op jit(solution)/shard_map/pallas_call | solution.py:282
  97.3 2.3 %dynamic-slice_bitcast_fusion = f32[256,1024]{1,0:T(8,128)} fusion(f32[4,256,1024]{2,1,0:T(8,128)} %shard_map.46, s32[]{:T(128)S(6)} %select_n.8), kind=kLoop, calls=%fused_computation | loop fusion | bytes 2097156 | tf_op jit(solution)/shard_map/jit(dynamic_index_in_dim)/squeeze | solution.py:321

commit v3 on v2

--- a/solution.py
+++ b/solution.py
@@ -219,19 +219,19 @@
         def _():
             add_x(-1)
 
+        @pl.when(jnp.logical_and(n >= LAG_Y + LAG_CORE, n < LAG_Y + LAG_CORE + steps))
+        def _():
+            add_core(n - LAG_Y - LAG_CORE)
+
+        @pl.when(n >= LAG_Y + LAG_CORE + LAG_X)
+        def _():
+            add_x(n - LAG_Y - LAG_CORE - LAG_X)
+
         @pl.when(jnp.logical_and(n >= LAG_Y, n < LAG_Y + steps))
         def _():
             p = n - LAG_Y
             to_y(slot_of(p), lax.rem(p, chunks)).wait_recv()
             multiply(p)
-
-        @pl.when(jnp.logical_and(n >= LAG_Y + LAG_CORE, n < LAG_Y + LAG_CORE + steps))
-        def _():
-            add_core(n - LAG_Y - LAG_CORE)
-
-        @pl.when(n >= LAG_Y + LAG_CORE + LAG_X)
-        def _():
-            add_x(n - LAG_Y - LAG_CORE - LAG_X)
 
         return carry
 

time: 99.9 us -> 98.4 us (0.985)
  Pallas kernels: 93.5 us -> 92.1 us
    pallas_call x1, Pallas kernels: 93.5 us -> 92.1 us  [all_slots_owned(): pl.pallas_call(slot_kernel, out_shape=jax.ShapeDtypeStruct((slots, rows,...]
where the time goes in v3:
time: 98.4 us; the launch traced here: 98.3 us
  Pallas kernels  92.1 us (94%)
  local copies, waits for them, and re-layouts  3.55 us (4%)
  between operations  2.6 us (3%)
    pallas_call x1, Pallas kernels, all_slots_owned(): pl.pallas_call(slot_kernel, out_shape=jax.ShapeDtypeStruct((slots, rows,...  92.1 us
    squeeze x1, local copies, waits for them, and re-layouts, all_slots_owned(): lax.dynamic_index_in_dim(scores, owners[lax.axis_index('ckpt')], 0, keepd...  2.31 us

profile of v3, /device:TPU:17, one launch (start us, length us, event | category | flops | bytes accessed | tf_op | source)
XLA Modules:
  0.0 98.3 jit_solution(10370270701286598770)
XLA Ops:
  0.7 1.2 %dynamic_slice.7 = s32[1]{0:T(128)} dynamic-slice(s32[4]{0:T(128)} %param.6, s32[]{:T(128)S(6)} %select_n.7), dynamic_slice_sizes={1} | dynamic-slice | bytes 12 | tf_op jit(solution)/shard_map/dynamic_slice | solution.py:321
  3.8 92.1 %shard_map.46 = f32[4,256,1024]{2,1,0:T(8,128)} custom-call(bf16[1024,4096]{1,0:T(8,128)(2,1)} %bitcast.5, bf16[256,4096]{1,0:T(8,128)(2,1)} %bitcast.6, f32[1]{0:T(128)S(6)} %copy.5.weight_ref), custom_call_target="tpu_custom_call" | custom-call | flops 8589934592 | bytes 16777216 | tf_op jit(solution)/shard_map/pallas_call | solution.py:282
  95.9 2.3 %dynamic-slice_bitcast_fusion = f32[256,1024]{1,0:T(8,128)} fusion(f32[4,256,1024]{2,1,0:T(8,128)} %shard_map.46, s32[]{:T(128)S(6)} %select_n.8), kind=kLoop, calls=%fused_computation | loop fusion | bytes 2097156 | tf_op jit(solution)/shard_map/jit(dynamic_index_in_dim)/squeeze | solution.py:321
